TPU v7x, 32 devices: a whole 2x2x4 slice. The times are simulated.
32 devices in a mesh: dp: 8 (over y, x, core), rep: 4 (over z).
Axes of the slice: x: 2, y: 2, z: 4, core: 2. Of those that a mesh axis runs over, the one named last changes fastest.
Arguments:
- clips: bfloat16 [32, 1024, 256], P(('dp', 'rep')), may hold values from -6 to 6
- cotangent: bfloat16 [32, 1024, 256], P(('dp', 'rep')), may hold values from -0.59765625 to 0.59765625
- alphas: float32 [2, 256], replicated, may hold values from 0.5 to 4
- weights: bfloat16 [524288], replicated, may hold values from -0.125 to 0.125
- master: float32 [524288], P('dp'), may hold values from -2 to 2
- first_moment: float32 [524288], P('dp'), may hold values from -6 to 6
- second_moment: float32 [524288], P('dp'), may hold values from 0.05 to 2
Outputs:
- new_weights: bfloat16 [524288], replicated
- new_master: float32 [524288], P('dp')
- new_first: float32 [524288], P('dp')
- new_second: float32 [524288], P('dp')
All inputs are finite; a program needn't handle non-finite values.
Results may differ from a plain program's by a relative error of at most 0.0013.
Values may be sent and summed in bfloat16 or wider, within the bound.
A program may use at most 64 MiB of HBM per device.

v0:
```python
import jax
import jax.numpy as jnp
from jax import lax
from jax.sharding import PartitionSpec as P

CH = 256
TAPS = 7
DILATION = 3


BIAS_ONE = 0.9999734386011124
BIAS_TWO = 0.09520785288629041


def snake(values, alpha):
    return values + jnp.sin(alpha * values) ** 2 / alpha


def clip_grads(clip, cot, alphas, weights):
    split = TAPS * CH * CH
    frames = clip.shape[0]
    w_dilated = weights[:split].reshape(TAPS * CH, CH)
    w_point = weights[split:].reshape(CH, CH)
    first = snake(clip.astype(jnp.float32), alphas[0]).astype(jnp.bfloat16)
    reach = DILATION * (TAPS // 2)
    padded = jnp.pad(first, ((reach, reach), (0, 0)))
    windows = jnp.concatenate(
        [padded[k * DILATION : k * DILATION + frames] for k in range(TAPS)], axis=1
    )
    hidden = jnp.dot(windows, w_dilated, preferred_element_type=jnp.float32)
    second = snake(hidden, alphas[1]).astype(jnp.bfloat16)
    point_grad = jnp.dot(second.T, cot, preferred_element_type=jnp.float32)
    back = jnp.dot(cot, w_point.T, preferred_element_type=jnp.float32)
    d_hidden = (back * (1.0 + jnp.sin(2.0 * alphas[1] * hidden))).astype(jnp.bfloat16)
    dilated_grad = jnp.dot(windows.T, d_hidden, preferred_element_type=jnp.float32)
    return jnp.concatenate([dilated_grad.reshape(-1), point_grad.reshape(-1)])


def adam_update(gradient, master, first_moment, second_moment):
    new_first = 0.9 * first_moment + 0.1 * gradient
    new_second = 0.999 * second_moment + 0.001 * gradient * gradient
    new_master = master - 0.001 * (new_first / BIAS_ONE) / (jnp.sqrt(new_second / BIAS_TWO) + 1e-08)
    return (new_master, new_first, new_second)


def shards(clips, cotangent, alphas, weights, master, first_moment, second_moment):
    local_grad = clip_grads(clips[0], cotangent[0], alphas, weights)
    block_sum = lax.psum_scatter(local_grad, "dp", scatter_dimension=0, tiled=True)
    gradient = lax.psum(block_sum, "rep")
    new_master, new_first, new_second = adam_update(gradient, master, first_moment, second_moment)
    new_weights = lax.all_gather(new_master.astype(jnp.bfloat16), "dp", axis=0, tiled=True)
    return (new_weights, new_master, new_first, new_second)


def solution(mesh):
    return jax.shard_map(
        shards,
        mesh=mesh,
        in_specs=(
            P(("dp", "rep"), None, None),
            P(("dp", "rep"), None, None),
            P(),
            P(),
            P("dp"),
            P("dp"),
            P("dp"),
        ),
        out_specs=(P(), P("dp"), P("dp"), P("dp")),
        check_vma=False,
    )
```

profile of v0, /device:TPU:1, one launch (start us, length us, event | category | flops | bytes accessed | tf_op | source)
XLA Modules:
  0.0 177.0 jit_solution(8520979425764700998)
XLA Ops:
  7.2 0.8 broadcast_multiply_fusion
  8.0 4.6 %fusion.4 = bf16[1024,256]{1,0:T(8,128)(2,1)S(1)} fusion(bf16[1,1024,256]{2,1,0:T(8,128)(2,1)} %param.7, f32[256]{0:T(256)S(1)} %bitcast.27), kind=kLoop, calls=%fused_computation.10 | loop fusion | flops 1572864 | bytes 1049600 | tf_op jit(solution)/shard_map/convert_element_type | solution.py:24
  12.6 0.9 slice_dynamic-update-slice_fusion.5
  13.6 1.0 slice_dynamic-update-slice_fusion.4
  14.6 0.9 slice_dynamic-update-slice_fusion.3
  15.5 4.3 %constant_dynamic-update-slice_fusion = bf16[1024,1792]{1,0:T(8,128)(2,1)} fusion(bf16[1024,1792]{1,0:T(8,128)(2,1)} %slice_dynamic-update-slice_fusion.3, f32[256]{0:T(256)S(1)} %bitcast.28, bf16[1,1024,256]{2,1,0:T(8,128)(2,1)S(1)} %copy-done.1), kind=kLoop, calls=%fused_computation.29 | loop fusion | flops 1572864 | bytes 1049600
  19.8 1.0 slice_dynamic-update-slice_fusion.2
  20.8 1.0 slice_dynamic-update-slice_fusion.1
  21.8 1.0 slice_dynamic-update-slice_fusion
  22.7 0.3 slice.63
  23.1 4.1 %fusion.17 = f32[1024,256]{1,0:T(8,128)} fusion(bf16[1024,1792]{1,0:T(8,128)(2,1)} %slice_dynamic-update-slice_fusion, bf16[1792,256]{1,0:T(8,128)(2,1)S(1)} %slice.63), kind=kOutput, calls=%fused_computation.33 | convolution fusion | flops 939524096 | bytes 5636096 | tf_op jit(solution)/shard_map/dot_general | solution.py:30
  27.2 6.7 %convolution_bitcast_fusion = f32[224,2,8,128]{3,2,1,0:T(8,128)S(1)} fusion(bf16[1024,1792]{1,0:T(8,128)(2,1)} %slice_dynamic-update-slice_fusion, bf16[256,256]{1,0:T(8,128)(2,1)S(1)} %slice.60, f32[1024,256]{1,0:T(8,128)} %fusion.17, bf16[1,1024,256]{2,1,0:T(8,128)(2,1)S(1)} %copy-done, f32[256]{0:T(256)S(1)} %bitcast.30), kind=kOutput, calls=%fused_computation.1 | convolution fusion | flops 1074790400 | bytes 7209984 | tf_op jit(solution)/shard_map/dot_general | solution.py:35
  33.9 0.9 copy.11
  34.9 0.3 copy-done.6
  35.1 3.9 %convolution_bitcast_fusion.1 = f32[32,2,8,128]{3,2,1,0:T(8,128)S(1)} fusion(bf16[1,1024,256]{2,1,0:T(8,128)(2,1)S(1)} %copy-done, f32[1024,256]{1,0:T(8,128)S(1)} %copy-done.6, f32[256]{0:T(256)S(1)} %bitcast.29), kind=kOutput, calls=%fused_computation.6 | convolution fusion | flops 135528448 | bytes 1836032 | tf_op jit(solution)/shard_map/dot_general | solution.py:32
  39.1 0.1 copy.12
  39.3 1.5 pad_maximum_fusion
  40.8 0.6 dynamic-slice
  42.1 61.3 %all-reduce.7.cloned.1.call-done = f32[524288]{0:T(1024)} async-done(((f32[524288]{0:T(1024)}), f32[524288]{0:T(1024)}) %all-reduce.7.cloned.1.call-update) | async-done | bytes 2097168
  103.4 1.7 dynamic-slice.1
  105.1 35.4 %all-reduce.5.cloned.1.call-done = f32[65536]{0:T(1024)} async-done(((f32[65536]{0:T(1024)}), f32[65536]{0:T(1024)}) %all-reduce.5.cloned.1.call-update) | async-done | bytes 262160 | tf_op jit(solution)/shard_map/psum | solution.py:49
  140.5 2.0 %fusion.15 = (bf16[65536]{0:T(1024)(128)(2,1)}, f32[65536]{0:T(1024)}, f32[65536]{0:T(1024)}, f32[65536]{0:T(1024)}) fusion(f32[65536]{0:T(1024)S(1)} %copy-done.2, f32[65536]{0:T(1024)} %all-reduce.5.cloned.1.call-done, f32[65536]{0:T(1024)S(1)} %copy-done.3, f32[65536]{0:T(1024)S(1)} %copy-done.4), kind=kLoop, calls=%fused_computation.32 | loop fusion | flops 851968 | bytes 1966080 | tf_op jit(solution)/shard_map/convert_element_type | solution.py:51
  142.5 25.7 %all-gather.2.cloned.1.call-done = bf16[524288]{0:T(1024)(128)(2,1)} async-done(((bf16[65536]{0:T(1024)(128)(2,1)}), bf16[524288]{0:T(1024)(128)(2,1)}) %all-gather.2.cloned.1.call-update) | async-done | bytes 1048592 | tf_op jit(solution)/shard_map/all_gather | solution.py:51
  168.2 2.3 %copy.22 = bf16[524288]{0:T(1024)(128)(2,1)} copy(bf16[524288]{0:T(1024)(128)(2,1)} %all-gather.2.cloned.1.call-done) | data formatting | bytes 2097152
  (24 shorter events, 0.3 us)
Async XLA Ops:
  7.2 20.1 %copy-start = (bf16[1,1024,256]{2,1,0:T(8,128)(2,1)S(1)}, bf16[1,1024,256]{2,1,0:T(8,128)(2,1)}, u32[]{:S(2)}) copy-start(bf16[1,1024,256]{2,1,0:T(8,128)(2,1)} %param.8) | copy-start | bytes 1572868
  7.2 8.3 %copy-start.1 = (bf16[1,1024,256]{2,1,0:T(8,128)(2,1)S(1)}, bf16[1,1024,256]{2,1,0:T(8,128)(2,1)}, u32[]{:S(2)}) copy-start(bf16[1,1024,256]{2,1,0:T(8,128)(2,1)} %param.7) | copy-start | bytes 1572868
  7.2 96.2 %all-reduce.7.cloned.1.call-start = ((), (), s32[]{:S(2)}) async-start(), calls=%async_computation.2 | async-start | bytes 4194304
  12.6 10.1 %slice-start = ((bf16[524288]{0:T(1024)(128)(2,1)}), bf16[458752]{0:T(1024)(128)(2,1)S(1)}, s32[]{:S(2)}) async-start(bf16[524288]{0:T(1024)(128)(2,1)} %param.10), calls=%async_computation.3 | async-start | bytes 1835008 | tf_op jit(solution)/shard_map/slice | solution.py:22
  14.6 8.5 %slice-start.1 = ((bf16[524288]{0:T(1024)(128)(2,1)}), bf16[65536]{0:T(1024)(128)(2,1)S(1)}, s32[]{:S(2)}) async-start(bf16[524288]{0:T(1024)(128)(2,1)} %param.10), calls=%async_computation.4 | async-start | bytes 262144 | tf_op jit(solution)/shard_map/slice | solution.py:23
  33.9 1.2 copy-start.6
  39.1 1.7 copy-start.5
  39.2 101.3 %copy-start.2 = (f32[65536]{0:T(1024)S(1)}, f32[65536]{0:T(1024)}, u32[]{:S(2)}) copy-start(f32[65536]{0:T(1024)} %param.11) | copy-start | bytes 786436
  39.2 101.3 %copy-start.3 = (f32[65536]{0:T(1024)S(1)}, f32[65536]{0:T(1024)}, u32[]{:S(2)}) copy-start(f32[65536]{0:T(1024)} %param.12) | copy-start | bytes 786436
  39.3 101.3 %copy-start.4 = (f32[65536]{0:T(1024)S(1)}, f32[65536]{0:T(1024)}, u32[]{:S(2)}) copy-start(f32[65536]{0:T(1024)} %param.13) | copy-start | bytes 786436
  40.8 99.8 %all-reduce.5.cloned.1.call-start = ((), (), s32[]{:S(2)}) async-start(), calls=%async_computation | async-start | bytes 524288 | tf_op jit(solution)/shard_map/psum | solution.py:49
  105.1 63.2 %all-gather.2.cloned.1.call-start = ((), (), s32[]{:S(2)}) async-start(), calls=%async_computation.1 | async-start | bytes 1179648 | tf_op jit(solution)/shard_map/all_gather | solution.py:51
Sparse Core Ops, SparseCore 0:
  40.9 62.4 all-reduce.6
  106.3 34.1 all-reduce.4
  143.2 25.0 all-gather.1
where the time goes:
time: 178 us; the launch traced here: 177 us
  waiting for transfers between devices  122 us (69%)
  matrix products  14.7 us (8%)
  between operations  14.5 us (8%)
  other arithmetic  13.1 us (7%)
  local copies, waits for them, and re-layouts  12 us (7%)
    unnamed x4, waiting for transfers between devices  61.4 us
    psum x1, waiting for transfers between devices, shards(): gradient = lax.psum(block_sum, 'rep')  35.4 us
    all_gather x1, waiting for transfers between devices, shards(): lax.all_gather(new_master.astype(jnp.bfloat16), 'dp', axis=0, tiled=True)  25.7 us
    unnamed x24, local copies, waits for them, and re-layouts  10.7 us
    dot_general x1, matrix products, clip_grads(): jnp.dot(windows.T, d_hidden, preferred_element_type=jnp.float32)  6.67 us
    convert_element_type x1, other arithmetic, clip_grads(): first = snake(clip.astype(jnp.float32), alphas[0]).astype(jnp.bfloat16)  4.57 us
    unnamed x1, other arithmetic  4.32 us
    dot_general x1, matrix products, clip_grads(): hidden = jnp.dot(windows, w_dilated, preferred_element_type=jnp.float32)  4.13 us
  transfers between devices with their start and end apart: 3, of which 3 were waited for; matrix products, arithmetic and copies ran while one was open for 0% of the time, Pallas kernels for 0%

commit v1 on v0

v1 whole, which is shorter than its diff:
```python
import functools

import jax
import jax.numpy as jnp
from jax import lax
from jax.experimental import pallas as pl
from jax.experimental.pallas import tpu as pltpu
from jax.sharding import PartitionSpec as P

TAPS = 7
DILATION = 3
LANES = 128

BIAS_ONE = 0.9999734386011124
BIAS_TWO = 0.09520785288629041

PI_A = 3.140625
PI_B = 9.67502593994140625e-4
PI_C = 1.509957990978376432e-7
INV_PI = 0.3183098861837907

SIN = (-0.16666659712791443, 0.008333083242177963, -0.00019810810044873506, 2.6083068860316416e-06)
COS = (-0.5, 0.04166664183139801, -0.001388839678838849, 2.4761575332377106e-05, -2.607200428883516e-07)


def reduced(u):
    k = jnp.round(u * INV_PI)
    return ((u - k * PI_A) - k * PI_B) - k * PI_C


def sin_of(r, r2):
    return r + r * (r2 * (SIN[0] + r2 * (SIN[1] + r2 * (SIN[2] + r2 * SIN[3]))))


def cos_of(r2):
    return 1.0 + r2 * (COS[0] + r2 * (COS[1] + r2 * (COS[2] + r2 * (COS[3] + r2 * COS[4]))))


def dot(a, b, dims):
    return lax.dot_general(a, b, (dims, ((), ())), preferred_element_type=jnp.float32)


def adam(gradient, master, first_moment, second_moment):
    new_first = 0.9 * first_moment + 0.1 * gradient
    new_second = 0.999 * second_moment + 0.001 * gradient * gradient
    new_master = master - 0.001 * (new_first / BIAS_ONE) / (jnp.sqrt(new_second / BIAS_TWO) + 1e-08)
    return new_master, new_first, new_second


def step_kernel(
    plan,
    clip_hbm, cot_hbm, alpha_ref, w_hbm, ma_hbm, m1_hbm, m2_hbm,
    ow_hbm, oma_hbm, om1_hbm, om2_hbm,
    clip, cot, w_lin, w32, w_mat, ma, m1, m2,
    padded, win, lhs, grad, pair_buf, xy_buf, acc, z_buf, full, nw,
    in_sem, out_sem, pair_s, pair_r, xy_s, xy_r, zr_s, zr_r, zg_s, zg_r,
    ag_s, ag_r, to_s, to_r,
):
    frames, ch, dp, rep, rows, transposed, parts = plan
    chips = dp // 2
    lin = rows * ch // LANES
    part = lin // parts
    me = lax.axis_index("dp")
    z = lax.axis_index("rep")
    core = me % 2
    g = me // 2
    partner = g * 2 + 1 - core

    loads = [
        pltpu.make_async_copy(s, d, in_sem.at[i])
        for i, (s, d) in enumerate(
            [(clip_hbm, clip), (w_hbm, w_lin), (cot_hbm, cot), (ma_hbm, ma), (m1_hbm, m1), (m2_hbm, m2)]
        )
    ]
    for c in loads:
        c.start()

    barrier = pltpu.get_barrier_semaphore()
    pl.semaphore_signal(barrier, inc=1, device_id={"dp": partner})
    for k in range(1, chips):
        pl.semaphore_signal(barrier, inc=1, device_id={"dp": (g + k) % chips * 2 + core})
    for k in range(1, rep):
        pl.semaphore_signal(barrier, inc=1, device_id={"rep": (z + k) % rep})

    reach = DILATION * (TAPS // 2)
    base = 16
    split = TAPS * ch

    loads[0].wait()
    for h in range(ch // LANES):
        cols = slice(h * LANES, (h + 1) * LANES)
        a0 = alpha_ref[0:1, cols]
        v = clip[:, cols].astype(jnp.float32)
        r = reduced(a0 * v)
        s = sin_of(r, r * r)
        padded[h, 0:base, :] = jnp.zeros((base, LANES), jnp.float32)
        padded[h, base + frames : base + frames + base, :] = jnp.zeros((base, LANES), jnp.float32)
        padded[h, base : base + frames, :] = v + s * s * (1.0 / a0)
    for k in range(TAPS):
        for h in range(ch // LANES):
            start = base + DILATION * k - reach
            win[:, k * ch + h * LANES : k * ch + (h + 1) * LANES] = padded[
                h, start : start + frames, :
            ].astype(jnp.bfloat16)

    loads[1].wait()
    w32[...] = w_lin[...].astype(jnp.float32)
    per = ch // LANES
    for h in range(per):
        w_mat[:, h * LANES : (h + 1) * LANES] = w32[pl.ds(h, split + ch, stride=per), :].astype(jnp.bfloat16)

    loads[2].wait()
    lhs[1] = cot[...].astype(jnp.float32).T.astype(jnp.bfloat16)

    a1 = alpha_ref[1:2, :]
    inv1 = 1.0 / a1
    chunk = 256

    def forward(c, carry):
        at = pl.ds(pl.multiple_of(c * chunk, chunk), chunk)
        hidden = dot(win[at, :split], w_mat[:split, :], ((1,), (0,)))
        back = dot(cot[at, :], w_mat[split:, :], ((1,), (1,)))
        r = reduced(a1 * hidden)
        r2 = r * r
        s = sin_of(r, r2)
        win[at, split : split + ch] = (hidden + s * s * inv1).astype(jnp.bfloat16)
        d_hidden = back * (1.0 + 2.0 * s * cos_of(r2))
        lhs[0, :, at] = d_hidden.astype(jnp.bfloat16).astype(jnp.float32).T.astype(jnp.bfloat16)
        return carry

    lax.fori_loop(0, frames // chunk, forward, 0)

    def block(b):
        return grad.at[pl.ds(pl.multiple_of(b * rows, rows), rows), :]

    def tile(t):
        side = t // TAPS
        part_of = win[:, pl.ds(pl.multiple_of(t * ch, ch), ch)]
        if transposed:
            value = dot(lhs[side], part_of, ((1,), (0,)))
        else:
            value = dot(lhs[side], part_of, ((1,), (0,))).T
        grad[pl.ds(pl.multiple_of(t * ch, ch), ch), :] = value

    if not transposed:
        lax.fori_loop(0, TAPS, lambda t, c: (tile(t), c)[1], 0)
        second = dot(lhs[1], win[:, split : split + ch], ((1,), (0,)))
        grad[split : split + ch, :] = second.T

    pl.semaphore_wait(barrier, chips + rep - 1)

    def chip_at(o):
        return (g + 1 + o) % chips

    def pair_copy(o):
        return pltpu.make_async_remote_copy(
            block(chip_at(o) * 2 + 1 - core), pair_buf.at[o], pair_s.at[o], pair_r.at[o],
            device_id={"dp": partner},
        )

    def xy_copy(o):
        to = chip_at(o)
        return pltpu.make_async_remote_copy(
            block(to * 2 + core), xy_buf.at[o], xy_s.at[o], xy_r.at[o],
            device_id={"dp": to * 2 + core},
        )

    def produce(o, carry):
        i = chip_at(o)
        if transposed:
            tile(i * 2 + 1 - core)
        pair_copy(o).start()
        if transposed:
            tile(i * 2 + core)
        return carry

    lax.fori_loop(0, chips, produce, 0)

    def add_pair(o):
        pair_copy(o).wait_recv()
        b = chip_at(o) * 2 + core
        at = pl.ds(pl.multiple_of(b * rows, rows), rows)
        grad[at, :] = grad[at, :] + pair_buf[o]

    def send_on(o, carry):
        add_pair(o)
        xy_copy(o).start()
        return carry

    lax.fori_loop(0, chips - 1, send_on, 0)
    add_pair(chips - 1)

    def add_chip(o, total):
        xy_copy(o).wait_recv()
        return total + xy_buf[o]

    total = lax.fori_loop(
        0, chips - 1, add_chip, grad[pl.ds(pl.multiple_of(me * rows, rows), rows), :]
    )
    if transposed:
        total = total.T
    for h in range(per):
        acc[pl.ds(h, rows, stride=per), :] = total[:, h * LANES : (h + 1) * LANES]

    def z_peer(k):
        return (z + k) % rep

    def part_at(q):
        return pl.ds(pl.multiple_of(q * part, part), part)

    def zr_copy(k):
        src = acc.at[part_at(z_peer(k))] if parts > 1 else acc
        return pltpu.make_async_remote_copy(
            src, z_buf.at[k - 1 if parts > 1 else z], zr_s.at[k - 1], zr_r.at[k - 1],
            device_id={"rep": z_peer(k)},
        )

    def zr_wait(k):
        return pltpu.make_async_remote_copy(
            acc.at[part_at(0)] if parts > 1 else acc,
            z_buf.at[k - 1 if parts > 1 else (z + rep - k) % rep], zr_s.at[k - 1], zr_r.at[k - 1],
            device_id={"rep": z_peer(k)},
        )

    def zg_copy(k):
        at = part_at(z)
        return pltpu.make_async_remote_copy(
            full.at[at], full.at[at], zg_s.at[k - 1], zg_r.at[k - 1], device_id={"rep": z_peer(k)},
        )

    def zg_wait(k):
        at = part_at((z + rep - k) % rep)
        return pltpu.make_async_remote_copy(
            full.at[at], full.at[at], zg_s.at[k - 1], zg_r.at[k - 1], device_id={"rep": z_peer(k)},
        )

    for k in range(1, rep):
        zr_copy(k).start()
    if parts > 1:
        own = acc[part_at(z), :]
        for k in range(1, rep):
            zr_wait(k).wait_recv()
            own = own + z_buf[k - 1]
        full[part_at(z), :] = own
        for k in range(1, rep):
            zg_copy(k).start()
    else:
        z_buf[z] = acc[...]
        for k in range(1, rep):
            zr_wait(k).wait_recv()
        own = z_buf[0]
        for k in range(1, rep):
            own = own + z_buf[k]
        full[...] = own

    for c in loads[3:]:
        c.wait()

    def part_of(k):
        return (z + parts - k) % parts if parts > 1 else 0

    def place(owner, k):
        return ow_hbm.at[pl.ds(pl.multiple_of(owner * lin + part_of(k) * part, part), part), :]

    def outs(k):
        at = part_at(part_of(k))
        return [
            pltpu.make_async_copy(nw.at[at], place(me, k), out_sem.at[k, 0]),
            pltpu.make_async_copy(ma.at[at], oma_hbm.at[at], out_sem.at[k, 1]),
            pltpu.make_async_copy(m1.at[at], om1_hbm.at[at], out_sem.at[k, 2]),
            pltpu.make_async_copy(m2.at[at], om2_hbm.at[at], out_sem.at[k, 3]),
        ]

    def ag_copy(k, j):
        return pltpu.make_async_remote_copy(
            nw.at[part_at(part_of(k))], place(me, k), ag_s.at[k, j], ag_r.at[k, j],
            device_id={"dp": (g + j) % chips * 2 + core},
        )

    def ag_wait(k, j):
        at = place((g + chips - j) % chips * 2 + core, k)
        return pltpu.make_async_remote_copy(
            at, at, ag_s.at[k, j], ag_r.at[k, j], device_id={"dp": (g + j) % chips * 2 + core},
        )

    def to_copy(k, j):
        at = place((g + chips - j) % chips * 2 + core, k)
        src = nw.at[part_at(part_of(k))] if isinstance(j, int) and j == 0 else at
        return pltpu.make_async_remote_copy(
            src, at, to_s.at[k, j], to_r.at[k, j], device_id={"dp": partner},
        )

    def to_wait(k, j):
        at = place((g + chips - j) % chips * 2 + 1 - core, k)
        return pltpu.make_async_remote_copy(
            at, at, to_s.at[k, j], to_r.at[k, j], device_id={"dp": partner},
        )

    def loop(lo, hi, f):
        lax.fori_loop(lo, hi, lambda j, c: (f(j), c)[1], 0)

    for k in range(parts):
        if k > 0:
            zg_wait(k).wait_recv()
        at = part_at(part_of(k))
        new_master, new_first, new_second = adam(full[at, :], ma[at, :], m1[at, :], m2[at, :])
        nw[at, :] = new_master.astype(jnp.bfloat16)
        loop(1, chips, lambda j: ag_copy(k, j).start())
        to_copy(k, 0).start()
        ma[at, :] = new_master
        m1[at, :] = new_first
        m2[at, :] = new_second
        for c in outs(k):
            c.start()

    for k in range(parts):

        def hand_on(j):
            ag_wait(k, j).wait_recv()
            to_copy(k, j).start()

        loop(1, chips, hand_on)

    for k in range(parts):
        loop(0, chips, lambda j: to_wait(k, j).wait_recv())

    loop(0, chips, lambda o: pair_copy(o).wait_send())
    loop(0, chips - 1, lambda o: xy_copy(o).wait_send())
    for k in range(1, rep):
        zr_copy(k).wait_send()
        if parts > 1:
            zg_copy(k).wait_send()
    for k in range(parts):
        loop(1, chips, lambda j: ag_copy(k, j).wait_send())
        to_copy(k, 0).wait_send()
        loop(1, chips, lambda j: to_copy(k, j).wait_send())
        for c in outs(k):
            c.wait()


def shards(dp, rep, clips, cotangent, alphas, weights, master, first_moment, second_moment):
    frames, ch = clips.shape[1:]
    params = weights.shape[0]
    own = master.shape[0]
    rows = own // ch
    lin = own // LANES
    parts = rep if lin % (16 * rep) == 0 else 1
    part = lin // parts
    chips = dp // 2
    transposed = rows == ch
    plan = (frames, ch, dp, rep, rows, transposed, parts)
    anywhere = pl.BlockSpec(memory_space=pl.ANY)
    f32, bf16 = jnp.float32, jnp.bfloat16
    dma = pltpu.SemaphoreType.DMA
    outs = pl.pallas_call(
        functools.partial(step_kernel, plan),
        out_shape=(
            jax.ShapeDtypeStruct((params // LANES, LANES), bf16),
            jax.ShapeDtypeStruct((lin, LANES), f32),
            jax.ShapeDtypeStruct((lin, LANES), f32),
            jax.ShapeDtypeStruct((lin, LANES), f32),
        ),
        in_specs=[anywhere, anywhere, pl.BlockSpec(memory_space=pltpu.VMEM)] + [anywhere] * 4,
        out_specs=(anywhere,) * 4,
        scratch_shapes=[
            pltpu.VMEM((frames, ch), bf16),
            pltpu.VMEM((frames, ch), bf16),
            pltpu.VMEM((params // LANES, LANES), bf16),
            pltpu.VMEM((params // LANES, LANES), f32),
            pltpu.VMEM((params // ch, ch), bf16),
            pltpu.VMEM((lin, LANES), f32),
            pltpu.VMEM((lin, LANES), f32),
            pltpu.VMEM((lin, LANES), f32),
            pltpu.VMEM((ch // LANES, frames + 32, LANES), f32),
            pltpu.VMEM((frames, (TAPS + 1) * ch), bf16),
            pltpu.VMEM((2, ch, frames), bf16),
            pltpu.VMEM((params // ch, ch), f32),
            pltpu.VMEM((chips, rows, ch), f32),
            pltpu.VMEM((chips - 1, rows, ch), f32),
            pltpu.VMEM((lin, LANES), f32),
            pltpu.VMEM((rep, part, LANES), f32),
            pltpu.VMEM((lin, LANES), f32),
            pltpu.VMEM((lin, LANES), bf16),
            dma((6,)),
            dma((parts, 4)),
            dma((chips,)), dma((chips,)),
            dma((chips,)), dma((chips,)),
            dma((rep,)), dma((rep,)),
            dma((rep,)), dma((rep,)),
            dma((parts, chips)), dma((parts, chips)),
            dma((parts, chips)), dma((parts, chips)),
        ],
        compiler_params=pltpu.CompilerParams(
            collective_id=0, has_side_effects=True, vmem_limit_bytes=48 * 1024 * 1024
        ),
        name="train_step",
    )(
        clips[0],
        cotangent[0],
        alphas,
        weights.reshape(params // LANES, LANES),
        master.reshape(lin, LANES),
        first_moment.reshape(lin, LANES),
        second_moment.reshape(lin, LANES),
    )
    return tuple(o.reshape(-1) for o in outs)


def solution(mesh):
    return jax.shard_map(
        functools.partial(shards, mesh.shape["dp"], mesh.shape["rep"]),
        mesh=mesh,
        in_specs=(
            P(("dp", "rep"), None, None),
            P(("dp", "rep"), None, None),
            P(),
            P(),
            P("dp"),
            P("dp"),
            P("dp"),
        ),
        out_specs=(P(), P("dp"), P("dp"), P("dp")),
        check_vma=False,
    )
```

time: 178 us -> 55.7 us (0.31)
  waiting for transfers between devices: 122 us -> 0 us
  Pallas kernels: 0 us -> 44.6 us
  matrix products: 14.7 us -> 0 us
  between operations: 14.5 us -> 0.66 us
  other arithmetic: 13.1 us -> 0 us
  local copies, waits for them, and re-layouts: 12 us -> 10 us
    unnamed x4 -> x0, waiting for transfers between devices: 61.4 us -> none
    pallas_call x0 -> x1, Pallas kernels: none -> 44.6 us  [shards(): pl.pallas_call(functools.partial(step_kernel, plan), out_shape=(jax.Shape...]
    psum x1 -> x0, waiting for transfers between devices: 35.4 us -> none  [shards(): gradient = lax.psum(block_sum, 'rep')]
    all_gather x1 -> x0, waiting for transfers between devices: 25.7 us -> none  [shards(): lax.all_gather(new_master.astype(jnp.bfloat16), 'dp', axis=0, tiled=True)]
    dot_general x3 -> x0, matrix products: 14.7 us -> none  [the longest x1 6.67 us: clip_grads(): jnp.dot(windows.T, d_hidden, preferred_element_type=jnp.float32)]
    convert_element_type x2 -> x0, other arithmetic: 6.53 us -> none  [the longest x1 4.57 us: clip_grads(): first = snake(clip.astype(jnp.float32), alphas[0]).astype(jnp.bfloat16)]
    unnamed x1 -> x0, other arithmetic: 4.32 us -> none
    unnamed x24 -> x18, local copies, waits for them, and re-layouts: 10.7 us -> 10 us
  transfers between devices with their start and end apart: 3 -> 0, of which waited for: 3 -> 0; matrix products, arithmetic and copies ran while one was open for 0% -> 0% of each run, Pallas kernels for 0% -> 0%
where the time goes in v1:
time: 55.7 us; the launch traced here: 55.3 us
  Pallas kernels  44.6 us (80%)
  local copies, waits for them, and re-layouts  10 us (18%)
  between operations  0.66 us (1%)
    pallas_call x1, Pallas kernels, shards(): pl.pallas_call(functools.partial(step_kernel, plan), out_shape=(jax.Shape...  44.6 us
    unnamed x18, local copies, waits for them, and re-layouts  10 us

profile of v1, /device:TPU:1, one launch (start us, length us, event | category | flops | bytes accessed | tf_op | source)
XLA Modules:
  0.0 55.3 jit_solution(4781456359058858513)
XLA Ops:
  0.6 0.0 copy-start.6
  0.6 0.7 %copy-done.6 = f32[2,256]{1,0:T(2,128)S(1)} copy-done((f32[2,256]{1,0:T(2,128)S(1)}, f32[2,256]{1,0:T(2,128)}, u32[]{:S(2)}) %copy-start.6) | copy-done | bytes 2072
  1.3 0.0 copy-start
  1.3 1.2 %copy-done = bf16[524288]{0:T(1024)(128)(2,1)S(1)} copy-done((bf16[524288]{0:T(1024)(128)(2,1)S(1)}, bf16[524288]{0:T(1024)(128)(2,1)}, u32[]{:S(2)}) %copy-start) | copy-done | bytes 1048600
  2.5 0.0 copy-start.1
  2.5 1.0 %copy-done.1 = bf16[1,1024,256]{2,1,0:T(8,128)(2,1)S(1)} copy-done((bf16[1,1024,256]{2,1,0:T(8,128)(2,1)S(1)}, bf16[1,1024,256]{2,1,0:T(8,128)(2,1)}, u32[]{:S(2)}) %copy-start.1) | copy-done | bytes 524312
  3.6 0.0 copy-start.2
  3.6 1.0 %copy-done.2 = bf16[1,1024,256]{2,1,0:T(8,128)(2,1)S(1)} copy-done((bf16[1,1024,256]{2,1,0:T(8,128)(2,1)S(1)}, bf16[1,1024,256]{2,1,0:T(8,128)(2,1)}, u32[]{:S(2)}) %copy-start.2) | copy-done | bytes 524312
  4.6 0.0 copy-start.3
  4.6 0.9 %copy-done.3 = f32[65536]{0:T(1024)S(1)} copy-done((f32[65536]{0:T(1024)S(1)}, f32[65536]{0:T(1024)}, u32[]{:S(2)}) %copy-start.3) | copy-done | bytes 262168
  5.6 0.0 copy-start.4
  5.6 0.9 %copy-done.4 = f32[65536]{0:T(1024)S(1)} copy-done((f32[65536]{0:T(1024)S(1)}, f32[65536]{0:T(1024)}, u32[]{:S(2)}) %copy-start.4) | copy-done | bytes 262168
  6.5 0.0 copy-start.5
  6.5 0.9 %copy-done.5 = f32[65536]{0:T(1024)S(1)} copy-done((f32[65536]{0:T(1024)S(1)}, f32[65536]{0:T(1024)}, u32[]{:S(2)}) %copy-start.5) | copy-done | bytes 262168
  7.5 44.6 %train_step.1 = (bf16[4096,128]{1,0:T(8,128)(2,1)S(1)}, f32[512,128]{1,0:T(8,128)S(1)}, f32[512,128]{1,0:T(8,128)S(1)}, f32[512,128]{1,0:T(8,128)S(1)}) custom-call(bf16[1024,256]{1,0:T(8,128)(2,1)S(1)} %bitcast.12, bf16[1024,256]{1,0:T(8,128)(2,1)S(1)} %bitcast.13, f32[2,256]{1,0:T(2,128)S(1)} %copy-done.6, bf16[4096,128]{1,0:T(8,128)(2,1)S(1)} %bitcast.10, ...), custom_call_target="tpu_custom_call" | custom-call | tf_op jit(solution)/shard_map/train_step/pallas_call | solution.py:355
  52.1 1.0 %copy.15 = bf16[524288]{0:T(1024)(128)(2,1)} copy(bf16[524288]{0:T(1024)(128)(2,1)S(1)} %bitcast.11) | data formatting | bytes 2097152
  53.1 0.7 %copy.16 = f32[65536]{0:T(1024)} copy(f32[65536]{0:T(1024)S(1)} %bitcast.19) | data formatting | bytes 524288
  53.9 0.7 %copy.17 = f32[65536]{0:T(1024)} copy(f32[65536]{0:T(1024)S(1)} %bitcast.18) | data formatting | bytes 524288
  54.6 0.7 %copy.18 = f32[65536]{0:T(1024)} copy(f32[65536]{0:T(1024)S(1)} %bitcast.17) | data formatting | bytes 524288
Async XLA Ops:
  0.6 0.7 %copy-start.6 = (f32[2,256]{1,0:T(2,128)S(1)}, f32[2,256]{1,0:T(2,128)}, u32[]{:S(2)}) copy-start(f32[2,256]{1,0:T(2,128)} %alpha_ref.1) | copy-start | bytes 6148
  1.3 1.2 %copy-start = (bf16[524288]{0:T(1024)(128)(2,1)S(1)}, bf16[524288]{0:T(1024)(128)(2,1)}, u32[]{:S(2)}) copy-start(bf16[524288]{0:T(1024)(128)(2,1)} %param.10) | copy-start | bytes 3145732
  2.5 1.0 %copy-start.1 = (bf16[1,1024,256]{2,1,0:T(8,128)(2,1)S(1)}, bf16[1,1024,256]{2,1,0:T(8,128)(2,1)}, u32[]{:S(2)}) copy-start(bf16[1,1024,256]{2,1,0:T(8,128)(2,1)} %param.7) | copy-start | bytes 1572868
  3.6 1.0 %copy-start.2 = (bf16[1,1024,256]{2,1,0:T(8,128)(2,1)S(1)}, bf16[1,1024,256]{2,1,0:T(8,128)(2,1)}, u32[]{:S(2)}) copy-start(bf16[1,1024,256]{2,1,0:T(8,128)(2,1)} %param.8) | copy-start | bytes 1572868
  4.6 0.9 %copy-start.3 = (f32[65536]{0:T(1024)S(1)}, f32[65536]{0:T(1024)}, u32[]{:S(2)}) copy-start(f32[65536]{0:T(1024)} %param.11) | copy-start | bytes 786436
  5.6 0.9 %copy-start.4 = (f32[65536]{0:T(1024)S(1)}, f32[65536]{0:T(1024)}, u32[]{:S(2)}) copy-start(f32[65536]{0:T(1024)} %param.12) | copy-start | bytes 786436
  6.5 0.9 %copy-start.5 = (f32[65536]{0:T(1024)S(1)}, f32[65536]{0:T(1024)}, u32[]{:S(2)}) copy-start(f32[65536]{0:T(1024)} %param.13) | copy-start | bytes 786436

commit v2 on v1

v2 whole, which is shorter than its diff:
```python
import functools

import jax
import jax.numpy as jnp
from jax import lax
from jax.experimental import pallas as pl
from jax.experimental.pallas import tpu as pltpu
from jax.sharding import PartitionSpec as P

TAPS = 7
DILATION = 3
LANES = 128
PIECES = 2

BIAS_ONE = 0.9999734386011124
BIAS_TWO = 0.09520785288629041

PI_A = 3.140625
PI_B = 9.67502593994140625e-4
PI_C = 1.509957990978376432e-7
INV_PI = 0.3183098861837907

SIN = (-0.16666659712791443, 0.008333083242177963, -0.00019810810044873506, 2.6083068860316416e-06)
COS = (-0.5, 0.04166664183139801, -0.001388839678838849, 2.4761575332377106e-05, -2.607200428883516e-07)


def reduced(u):
    k = jnp.round(u * INV_PI)
    return ((u - k * PI_A) - k * PI_B) - k * PI_C


def sin_of(r, r2):
    return r + r * (r2 * (SIN[0] + r2 * (SIN[1] + r2 * (SIN[2] + r2 * SIN[3]))))


def cos_of(r2):
    return 1.0 + r2 * (COS[0] + r2 * (COS[1] + r2 * (COS[2] + r2 * (COS[3] + r2 * COS[4]))))


def dot(a, b, dims):
    return lax.dot_general(a, b, (dims, ((), ())), preferred_element_type=jnp.float32)


def adam(gradient, master, first_moment, second_moment):
    new_first = 0.9 * first_moment + 0.1 * gradient
    new_second = 0.999 * second_moment + 0.001 * gradient * gradient
    new_master = master - 0.001 * (new_first / BIAS_ONE) / (jnp.sqrt(new_second / BIAS_TWO) + 1e-08)
    return new_master, new_first, new_second


def step_kernel(
    plan,
    clip_hbm, cot_hbm, alpha_hbm, w_hbm, ma_hbm, m1_hbm, m2_hbm,
    ow_hbm, oma_hbm, om1_hbm, om2_hbm,
    clip, cot, alpha_ref, w_lin, w32, w_mat, ma, m1, m2,
    padded, win, lhs, grad, pair_buf, xy_buf, acc, z_buf, full, nw,
    in_sem, out_sem, pair_s, pair_r, xy_s, xy_r, zr_s, zr_r, zg_s, zg_r,
    ag_s, ag_r, to_s, to_r,
):
    frames, ch, dp, rep, rows, transposed, chunks, parts = plan
    chips = dp // 2
    lin = rows * ch // LANES
    chunk_lin = lin // chunks
    part = chunk_lin // parts
    wide = ch // chunks
    me = lax.axis_index("dp")
    z = lax.axis_index("rep")
    core = me % 2
    g = me // 2
    partner = g * 2 + 1 - core

    loads = [
        pltpu.make_async_copy(s, d, in_sem.at[i])
        for i, (s, d) in enumerate(
            [(alpha_hbm, alpha_ref), (clip_hbm, clip), (w_hbm, w_lin), (cot_hbm, cot), (ma_hbm, ma), (m1_hbm, m1), (m2_hbm, m2)]
        )
    ]
    for c in loads:
        c.start()

    barrier = pltpu.get_barrier_semaphore()
    pl.semaphore_signal(barrier, inc=1, device_id={"dp": partner})
    for k in range(1, chips):
        pl.semaphore_signal(barrier, inc=1, device_id={"dp": (g + k) % chips * 2 + core})
    for k in range(1, rep):
        pl.semaphore_signal(barrier, inc=1, device_id={"rep": (z + k) % rep})

    reach = DILATION * (TAPS // 2)
    base = 16
    split = TAPS * ch

    loads[0].wait()
    loads[1].wait()
    for h in range(ch // LANES):
        cols = slice(h * LANES, (h + 1) * LANES)
        a0 = alpha_ref[0:1, cols]
        v = clip[:, cols].astype(jnp.float32)
        r = reduced(a0 * v)
        s = sin_of(r, r * r)
        padded[h, 0:base, :] = jnp.zeros((base, LANES), jnp.float32)
        padded[h, base + frames : base + frames + base, :] = jnp.zeros((base, LANES), jnp.float32)
        padded[h, base : base + frames, :] = v + s * s * (1.0 / a0)
    for k in range(TAPS):
        for h in range(ch // LANES):
            start = base + DILATION * k - reach
            win[:, k * ch + h * LANES : k * ch + (h + 1) * LANES] = padded[
                h, start : start + frames, :
            ].astype(jnp.bfloat16)

    loads[2].wait()
    w32[...] = w_lin[...].astype(jnp.float32)
    per = ch // LANES
    for h in range(per):
        w_mat[:, h * LANES : (h + 1) * LANES] = w32[pl.ds(h, split + ch, stride=per), :].astype(jnp.bfloat16)

    loads[3].wait()
    lhs[1] = cot[...].T

    a1 = alpha_ref[1:2, :]
    inv1 = 1.0 / a1
    chunk = 256

    def forward(c, carry):
        at = pl.ds(pl.multiple_of(c * chunk, chunk), chunk)
        hidden = dot(win[at, :split], w_mat[:split, :], ((1,), (0,)))
        back = dot(cot[at, :], w_mat[split:, :], ((1,), (1,)))
        r = reduced(a1 * hidden)
        r2 = r * r
        s = sin_of(r, r2)
        win[at, split : split + ch] = (hidden + s * s * inv1).astype(jnp.bfloat16)
        d_hidden = back * (1.0 + 2.0 * s * cos_of(r2))
        lhs[0, :, at] = d_hidden.astype(jnp.bfloat16).T
        return carry

    lax.fori_loop(0, frames // chunk, forward, 0)

    def block(b):
        return grad.at[pl.ds(pl.multiple_of(b * rows, rows), rows), :]

    def tile(t):
        side = t // TAPS
        part_of = win[:, pl.ds(pl.multiple_of(t * ch, ch), ch)]
        if transposed:
            value = dot(lhs[side], part_of, ((1,), (0,)))
        else:
            value = dot(lhs[side], part_of, ((1,), (0,))).T
        grad[pl.ds(pl.multiple_of(t * ch, ch), ch), :] = value

    if not transposed:
        lax.fori_loop(0, TAPS, lambda t, c: (tile(t), c)[1], 0)
        second = dot(lhs[1], win[:, split : split + ch], ((1,), (0,)))
        grad[split : split + ch, :] = second.T

    pl.semaphore_wait(barrier, chips + rep - 1)

    def chip_at(o):
        return (g + 1 + o) % chips

    def pair_copy(o):
        return pltpu.make_async_remote_copy(
            block(chip_at(o) * 2 + 1 - core), pair_buf.at[o], pair_s.at[o], pair_r.at[o],
            device_id={"dp": partner},
        )

    def xy_copy(s, o):
        to = chip_at(o)
        return pltpu.make_async_remote_copy(
            block(to * 2 + core).at[:, s * wide : (s + 1) * wide], xy_buf.at[s, o], xy_s.at[s, o], xy_r.at[s, o],
            device_id={"dp": to * 2 + core},
        )

    def produce(o, carry):
        i = chip_at(o)
        if transposed:
            tile(i * 2 + 1 - core)
        pair_copy(o).start()
        if transposed:
            tile(i * 2 + core)
        return carry

    lax.fori_loop(0, chips, produce, 0)

    def add_pair(o):
        pair_copy(o).wait_recv()
        b = chip_at(o) * 2 + core
        at = pl.ds(pl.multiple_of(b * rows, rows), rows)
        grad[at, :] = grad[at, :] + pair_buf[o]

    def loop(lo, hi, f):
        lax.fori_loop(lo, hi, lambda j, c: (f(j), c)[1], 0)

    def send_on(o):
        add_pair(o)
        xy_copy(0, o).start()

    def z_peer(k):
        return (z + k) % rep

    def part_at(s, q):
        return pl.ds(pl.multiple_of(s * chunk_lin + q * part, part), part)

    def zr_copy(s, k, wait=False):
        if parts > 1:
            src, slot = acc.at[part_at(s, z_peer(k))], k - 1
        else:
            src, slot = acc.at[part_at(s, 0)], (z + rep - k) % rep if wait else z
        return pltpu.make_async_remote_copy(
            src, z_buf.at[s, slot], zr_s.at[s, k - 1], zr_r.at[s, k - 1], device_id={"rep": z_peer(k)},
        )

    def zg_copy(s, k, wait=False):
        at = part_at(s, (z + rep - k) % rep if wait else z)
        return pltpu.make_async_remote_copy(
            full.at[at], full.at[at], zg_s.at[s, k - 1], zg_r.at[s, k - 1], device_id={"rep": z_peer(k)},
        )

    def sum_chips(s):
        def add_chip(o, total):
            xy_copy(s, o).wait_recv()
            return total + xy_buf[s, o]

        at = pl.ds(pl.multiple_of(me * rows, rows), rows)
        total = lax.fori_loop(0, chips - 1, add_chip, grad[at, s * wide : (s + 1) * wide])
        if transposed:
            total = total.T
        for h in range(per):
            acc[pl.ds(s * chunk_lin + h, chunk_lin // per, stride=per), :] = total[:, h * LANES : (h + 1) * LANES]
        for k in range(1, rep):
            zr_copy(s, k).start()

    def sum_replicas(s):
        if parts > 1:
            own = acc[part_at(s, z), :]
            for k in range(1, rep):
                zr_copy(s, k, True).wait_recv()
                own = own + z_buf[s, k - 1]
            full[part_at(s, z), :] = own
            for k in range(1, rep):
                zg_copy(s, k).start()
        else:
            z_buf[s, z] = acc[part_at(s, 0), :]
            for k in range(1, rep):
                zr_copy(s, k, True).wait_recv()
            own = z_buf[s, 0]
            for k in range(1, rep):
                own = own + z_buf[s, k]
            full[part_at(s, 0), :] = own

    def part_of(s, k):
        return part_at(s, (z + parts - k) % parts if parts > 1 else 0)

    def place(owner, s, k):
        q = (z + parts - k) % parts if parts > 1 else 0
        return ow_hbm.at[pl.ds(pl.multiple_of(owner * lin + s * chunk_lin + q * part, part), part), :]

    def outs(s, k):
        at = part_of(s, k)
        return [
            pltpu.make_async_copy(nw.at[at], place(me, s, k), out_sem.at[s, k, 0]),
            pltpu.make_async_copy(ma.at[at], oma_hbm.at[at], out_sem.at[s, k, 1]),
            pltpu.make_async_copy(m1.at[at], om1_hbm.at[at], out_sem.at[s, k, 2]),
            pltpu.make_async_copy(m2.at[at], om2_hbm.at[at], out_sem.at[s, k, 3]),
        ]

    def ag_copy(s, k, j, wait=False):
        if wait:
            src = dst = place((g + chips - j) % chips * 2 + core, s, k)
        else:
            src, dst = nw.at[part_of(s, k)], place(me, s, k)
        return pltpu.make_async_remote_copy(
            src, dst, ag_s.at[s, k, j], ag_r.at[s, k, j], device_id={"dp": (g + j) % chips * 2 + core},
        )

    def to_copy(s, k, j):
        at = place((g + chips - j) % chips * 2 + core, s, k)
        src = nw.at[part_of(s, k)] if isinstance(j, int) and j == 0 else at
        return pltpu.make_async_remote_copy(
            src, at, to_s.at[s, k, j], to_r.at[s, k, j], device_id={"dp": partner},
        )

    def to_wait(s, k, j):
        at = place((g + chips - j) % chips * 2 + 1 - core, s, k)
        return pltpu.make_async_remote_copy(
            at, at, to_s.at[s, k, j], to_r.at[s, k, j], device_id={"dp": partner},
        )

    def update(s, k):
        if k > 0:
            zg_copy(s, k, True).wait_recv()
        at = part_of(s, k)
        new_master, new_first, new_second = adam(full[at, :], ma[at, :], m1[at, :], m2[at, :])
        nw[at, :] = new_master.astype(jnp.bfloat16)
        loop(1, chips, lambda j: ag_copy(s, k, j).start())
        to_copy(s, k, 0).start()
        ma[at, :] = new_master
        m1[at, :] = new_first
        m2[at, :] = new_second
        for c in outs(s, k):
            c.start()

    def hand_on(s, k):
        def one(j):
            ag_copy(s, k, j, True).wait_recv()
            to_copy(s, k, j).start()

        loop(1, chips, one)

    loop(0, chips - 1, send_on)
    add_pair(chips - 1)
    for s in range(1, chunks):
        loop(0, chips - 1, lambda o: xy_copy(s, o).start())
    for c in loads[4:]:
        c.wait()

    sum_chips(0)
    sum_replicas(0)
    update(0, 0)
    for s in range(1, chunks):
        sum_chips(s)
        for k in range(1, parts):
            update(s - 1, k)
        sum_replicas(s)
        update(s, 0)
        for k in range(parts):
            hand_on(s - 1, k)
    for k in range(1, parts):
        update(chunks - 1, k)
    for k in range(parts):
        hand_on(chunks - 1, k)

    for s in range(chunks):
        for k in range(parts):
            loop(0, chips, lambda j: to_wait(s, k, j).wait_recv())

    loop(0, chips, lambda o: pair_copy(o).wait_send())
    for s in range(chunks):
        loop(0, chips - 1, lambda o: xy_copy(s, o).wait_send())
        for k in range(1, rep):
            zr_copy(s, k).wait_send()
            if parts > 1:
                zg_copy(s, k).wait_send()
        for k in range(parts):
            loop(1, chips, lambda j: ag_copy(s, k, j).wait_send())
            to_copy(s, k, 0).wait_send()
            loop(1, chips, lambda j: to_copy(s, k, j).wait_send())
            for c in outs(s, k):
                c.wait()


def results_kernel(*refs):
    half = len(refs) // 2
    sem = refs[-1]
    copies = []
    for i, (src, dst) in enumerate(zip(refs[:half], refs[half:-1])):
        n = src.shape[0] // PIECES
        for p in range(PIECES):
            at = pl.ds(p * n, n)
            copies.append(pltpu.make_async_copy(src.at[at], dst.at[at], sem.at[i, p]))
    for c in copies:
        c.start()
    for c in copies:
        c.wait()


def shards(dp, rep, clips, cotangent, alphas, weights, master, first_moment, second_moment):
    frames, ch = clips.shape[1:]
    params = weights.shape[0]
    own = master.shape[0]
    rows = own // ch
    lin = own // LANES
    chips = dp // 2
    transposed = rows == ch
    chunks = ch // LANES if transposed else 1
    parts = rep if lin // chunks % (16 * rep) == 0 else 1
    part = lin // chunks // parts
    plan = (frames, ch, dp, rep, rows, transposed, chunks, parts)
    anywhere = pl.BlockSpec(memory_space=pl.ANY)
    f32, bf16 = jnp.float32, jnp.bfloat16
    dma = pltpu.SemaphoreType.DMA
    outs = pl.pallas_call(
        functools.partial(step_kernel, plan),
        out_shape=(
            jax.ShapeDtypeStruct((params // LANES, LANES), bf16),
            jax.ShapeDtypeStruct((lin, LANES), f32),
            jax.ShapeDtypeStruct((lin, LANES), f32),
            jax.ShapeDtypeStruct((lin, LANES), f32),
        ),
        in_specs=[anywhere] * 7,
        out_specs=(anywhere,) * 4,
        scratch_shapes=[
            pltpu.VMEM((frames, ch), bf16),
            pltpu.VMEM((frames, ch), bf16),
            pltpu.VMEM(alphas.shape, f32),
            pltpu.VMEM((params // LANES, LANES), bf16),
            pltpu.VMEM((params // LANES, LANES), f32),
            pltpu.VMEM((params // ch, ch), bf16),
            pltpu.VMEM((lin, LANES), f32),
            pltpu.VMEM((lin, LANES), f32),
            pltpu.VMEM((lin, LANES), f32),
            pltpu.VMEM((ch // LANES, frames + 32, LANES), f32),
            pltpu.VMEM((frames, (TAPS + 1) * ch), bf16),
            pltpu.VMEM((2, ch, frames), bf16),
            pltpu.VMEM((params // ch, ch), f32),
            pltpu.VMEM((chips, rows, ch), f32),
            pltpu.VMEM((chunks, chips - 1, rows, ch // chunks), f32),
            pltpu.VMEM((lin, LANES), f32),
            pltpu.VMEM((chunks, rep, part, LANES), f32),
            pltpu.VMEM((lin, LANES), f32),
            pltpu.VMEM((lin, LANES), bf16),
            dma((7,)),
            dma((chunks, parts, 4)),
            dma((chips,)), dma((chips,)),
            dma((chunks, chips)), dma((chunks, chips)),
            dma((chunks, rep)), dma((chunks, rep)),
            dma((chunks, rep)), dma((chunks, rep)),
            dma((chunks, parts, chips)), dma((chunks, parts, chips)),
            dma((chunks, parts, chips)), dma((chunks, parts, chips)),
        ],
        compiler_params=pltpu.CompilerParams(
            collective_id=0, has_side_effects=True, vmem_limit_bytes=64 * 1024 * 1024
        ),
        name="train_step",
    )(
        clips[0],
        cotangent[0],
        alphas,
        weights.reshape(params // LANES, LANES),
        master.reshape(lin, LANES),
        first_moment.reshape(lin, LANES),
        second_moment.reshape(lin, LANES),
    )
    outs = pl.pallas_call(
        results_kernel,
        out_shape=tuple(jax.ShapeDtypeStruct(o.shape, o.dtype) for o in outs),
        in_specs=[anywhere] * len(outs),
        out_specs=(anywhere,) * len(outs),
        scratch_shapes=[dma((len(outs), PIECES))],
        compiler_params=pltpu.CompilerParams(vmem_limit_bytes=64 * 1024 * 1024),
        name="results",
    )(*outs)
    return tuple(o.reshape(-1) for o in outs)


def solution(mesh):
    return jax.shard_map(
        functools.partial(shards, mesh.shape["dp"], mesh.shape["rep"]),
        mesh=mesh,
        in_specs=(
            P(("dp", "rep"), None, None),
            P(("dp", "rep"), None, None),
            P(),
            P(),
            P("dp"),
            P("dp"),
            P("dp"),
        ),
        out_specs=(P(), P("dp"), P("dp"), P("dp")),
        check_vma=False,
    )
```

time: 55.7 us -> 102 us (1.83)
  Pallas kernels: 44.6 us -> 101 us
  local copies, waits for them, and re-layouts: 10 us -> 0 us
    pallas_call x0 -> x1, Pallas kernels: none -> 56.8 us  [shards(): pl.pallas_call(results_kernel, out_shape=tuple((jax.ShapeDtypeStruct(o.sh...]
    unnamed x18 -> x0, local copies, waits for them, and re-layouts: 10 us -> none
where the time goes in v2:
time: 102 us
  Pallas kernels  101 us (99%)
    pallas_call x1, Pallas kernels, shards(): pl.pallas_call(results_kernel, out_shape=tuple((jax.ShapeDtypeStruct(o.sh...  56.8 us
    pallas_call x1, Pallas kernels, shards(): pl.pallas_call(functools.partial(step_kernel, plan), out_shape=(jax.Shape...  44.2 us

profile of v2, /device:TPU:1, one launch (start us, length us, event | category | flops | bytes accessed | tf_op | source)
XLA Modules:
  0.0 101.6 jit_solution(10614288808207940915)
XLA Ops:
  0.6 44.2 %train_step.1 = (bf16[4096,128]{1,0:T(8,128)(2,1)}, f32[512,128]{1,0:T(8,128)}, f32[512,128]{1,0:T(8,128)}, f32[512,128]{1,0:T(8,128)}) custom-call(bf16[1024,256]{1,0:T(8,128)(2,1)} %bitcast.11, bf16[1024,256]{1,0:T(8,128)(2,1)} %bitcast.12, f32[2,256]{1,0:T(2,128)} %alpha_hbm.1, bf16[4096,128]{1,0:T(8,128)(2,1)} %bitcast.10, f32[512,128]{1,0:T(8,128)} %bitcast.13, ...), custom_call_target="tpu_custom_call" | custom-call | tf_op jit(solution)/shard_map/train_step/pallas_call | solution.py:380
  44.8 56.8 %results.1 = (bf16[4096,128]{1,0:T(8,128)(2,1)}, f32[512,128]{1,0:T(8,128)}, f32[512,128]{1,0:T(8,128)}, f32[512,128]{1,0:T(8,128)}) custom-call(bf16[4096,128]{1,0:T(8,128)(2,1)} %get-tuple-element.12.refs_0_, f32[512,128]{1,0:T(8,128)} %get-tuple-element.13.refs_1_, f32[512,128]{1,0:T(8,128)} %get-tuple-element.14.refs_2_, ...), custom_call_target="tpu_custom_call" | custom-call | tf_op jit(solution)/shard_map/results/pallas_call | solution.py:432
